TPU v7x, 256 devices: a whole 4x4x8 slice. The times are simulated.
256 devices in a mesh: replica: 16 (over y, z_lo), fsdp: 16 (over x, z_hi, core).
Axes of the slice: x: 4, y: 4, z: 8 (z_hi: 2, z_lo: 4; z = z_hi * 4 + z_lo), core: 2. Of those that a mesh axis runs over, the one named last changes fastest.
Arguments:
- local_weights: float32 [16, 5120, 512], P('replica', 'fsdp')
- outer_base: float32 [5120, 512], P('fsdp')
- outer_momentum: float32 [5120, 512], P(('fsdp', 'replica')), may hold values from -4 to 4
- batch: bfloat16 [16, 2, 6144, 5120], P('replica', None, 'fsdp'), may hold values from -6 to 6
- cotangent: bfloat16 [16, 2, 6144, 512], P('replica', None, 'fsdp'), may hold values from -6 to 6
- step: int32 [1], replicated, may hold values from 0 to 4095
- plan: int32 [8], replicated, may hold values from 0 to 3
Outputs:
- new_weights: float32 [16, 5120, 512], P('replica', 'fsdp')
- new_base: float32 [5120, 512], P('fsdp')
- new_momentum: float32 [5120, 512], P(('fsdp', 'replica'))
All inputs are finite; a program needn't handle non-finite values. Where the computation divides by a largest or mean magnitude, that divisor is 1e-20 or more.
Results may differ from a plain program's by a relative error of at most 0.0055.
Values may be sent and summed in bfloat16 or wider, within the bound.
No kernel may reach another device: no remote copies, remote signals or barrier semaphores. Data moves between devices by JAX's collectives and lax.ppermute only.
A program may use at most 128 MiB of HBM per device.

v0:
```python
import jax
import jax.numpy as jnp
from jax import lax
from jax.sharding import PartitionSpec as P

D = 5120
HEAD_DIM = 128
SCHED_LEN = 8
INNER = 2
eps_norm = 1e-06
eps_scale = 1e-06
inner_rate = 0.5
outer_rate = 0.7
outer_decay = 0.9
mix_local = 0.5


def pick_fragment(step, plan):
    position = step[0] % SCHED_LEN
    hits = jnp.arange(SCHED_LEN, dtype=jnp.int32) == position
    return jnp.sum(jnp.where(hits, plan, 0))


def rate_of(step):
    return outer_rate * 1024.0 / (1024.0 + step[0].astype(jnp.float32))


def normalize(rows):
    values = rows.astype(jnp.float32)
    mean_square = jnp.mean(values * values, axis=-1, keepdims=True)
    return (values * lax.rsqrt(mean_square + eps_norm)).astype(jnp.bfloat16)


def silu_slope(values):
    gate_value = jax.nn.sigmoid(values)
    return gate_value * (1.0 + values * (1.0 - gate_value))


def on_device(local_weights, outer_base, outer_momentum, batch, cotangent, step, plan):
    inv_width = D ** (-0.5)
    fragment = pick_fragment(step, plan)
    outer_lr = rate_of(step)
    first_col = fragment * HEAD_DIM
    weights = local_weights[0]
    base_cols = lax.dynamic_slice_in_dim(outer_base, first_col, HEAD_DIM, 1)
    pseudo_grad = base_cols - lax.dynamic_slice_in_dim(weights, first_col, HEAD_DIM, 1)
    block_scale = (jnp.max(jnp.abs(pseudo_grad), axis=1) + eps_scale).astype(jnp.bfloat16)
    codes_out = (pseudo_grad / block_scale.astype(jnp.float32)[:, None]).astype(jnp.bfloat16)
    moment_cols = lax.dynamic_slice_in_dim(outer_momentum, first_col, HEAD_DIM, 1)
    share_rows = moment_cols.shape[0]
    share_first = lax.axis_index("replica") * share_rows
    replicas = lax.axis_size("replica")
    dequant = (
        lax.all_gather(codes_out[None], "replica", axis=0, tiled=True).astype(jnp.float32)
        * lax.all_gather(block_scale[None], "replica", axis=0, tiled=True).astype(jnp.float32)[
            :, :, None
        ]
    )
    running = jnp.sum(dequant, axis=0)
    average = running / replicas
    moment_all = lax.all_gather(moment_cols, "replica", axis=0, tiled=True)
    moment_full = outer_decay * moment_all + average
    base_frag = base_cols - outer_lr * (outer_decay * moment_full + average)
    moment_new = lax.dynamic_slice_in_dim(moment_full, share_first, share_rows, 0)
    for index in range(INNER):
        normed = normalize(batch[0, index])
        cot_rows = cotangent[0, index].astype(jnp.float32)
        values = (
            jnp.dot(
                normed,
                lax.all_gather(weights.astype(jnp.bfloat16), "fsdp", axis=0, tiled=True),
                preferred_element_type=jnp.float32,
            )
            * inv_width
        )
        slopes = (cot_rows * silu_slope(values)).astype(jnp.bfloat16)
        gradient = lax.psum_scatter(
            jnp.dot(normed.T, slopes, preferred_element_type=jnp.float32).astype(jnp.bfloat16),
            "fsdp",
            scatter_dimension=0,
            tiled=True,
        ).astype(jnp.float32)
        weights = weights - inner_rate * inv_width * gradient
    trained_cols = lax.dynamic_slice_in_dim(weights, first_col, HEAD_DIM, 1)
    blended = mix_local * trained_cols + (1.0 - mix_local) * base_frag
    new_weights = lax.dynamic_update_slice_in_dim(weights, blended, first_col, 1)[None]
    new_base = lax.dynamic_update_slice_in_dim(outer_base, base_frag, first_col, 1)
    new_momentum = lax.dynamic_update_slice_in_dim(outer_momentum, moment_new, first_col, 1)
    return (new_weights, new_base, new_momentum)


def solution(mesh):
    placed = (
        P("replica", "fsdp", None),
        P("fsdp", None),
        P(("fsdp", "replica"), None),
        P("replica", None, "fsdp", None),
        P("replica", None, "fsdp", None),
        P(),
        P(),
    )
    return jax.shard_map(
        on_device,
        mesh=mesh,
        in_specs=placed,
        out_specs=(P("replica", "fsdp", None), P("fsdp", None), P(("fsdp", "replica"), None)),
        check_vma=False,
    )
```

profile of v0, /device:TPU:8, one launch (start us, length us, event | category | flops | bytes accessed | tf_op | source)
XLA Modules:
  0.0 509.7 jit_solution(3439085764657868025)
XLA Ops:
  7.2 0.0 copy-start.5
  7.2 0.0 all-gather.7.cloned.1.call-start
  7.2 1.2 copy.17
  8.4 0.8 copy.18
  9.2 1.9 bitcast_convert_fusion
  11.0 0.0 all-gather.7.cloned.1.call-update
  11.0 0.0 reduce-scatter.3.cloned.1.call-start
  11.1 4.2 fusion
  15.3 83.7 %all-gather.7.cloned.1.call-done = bf16[5120,512]{1,0:T(8,128)(2,1)} async-done(((bf16[320,512]{1,0:T(8,128)(2,1)}), bf16[5120,512]{1,0:T(8,128)(2,1)}) %all-gather.7.cloned.1.call-update) | async-done | bytes 5242896 | tf_op jit(solution)/shard_map/all_gather | solution.py:71
  99.0 0.0 copy-done.5
  99.0 12.4 %convolution_convert_fusion.1 = bf16[5120,512]{1,0:T(8,128)(2,1)} fusion(f32[384]{0:T(512)S(1)} %add_rsqrt_fusion.1, bf16[1,2,384,5120]{3,2,1,0:T(8,128)(2,1)} %param.10, bf16[5120,512]{1,0:T(8,128)(2,1)} %all-gather.7.cloned.1.call-done, bf16[1,2,384,512]{3,2,1,0:T(8,128)(2,1)S(1)} %copy-done.5), kind=kOutput, calls=%fused_computation.9 | convolution fusion | flops 4043112448 | bytes 18747392 | tf_op jit(solution)/shard_map/dot_general | solution.py:78
  111.4 0.0 copy-start
  111.4 0.0 copy-start.6
  111.4 0.0 reduce-scatter.3.cloned.1.call-update
  111.4 0.0 all-gather.9.cloned.1.call-start
  111.5 107.9 %reduce-scatter.3.cloned.1.call-done = bf16[320,512]{1,0:T(8,128)(2,1)} async-done(((bf16[5120,512]{1,0:T(8,128)(2,1)}), bf16[320,512]{1,0:T(8,128)(2,1)}) %reduce-scatter.3.cloned.1.call-update) | async-done | bytes 327696 | tf_op jit(solution)/shard_map/reduce_scatter | solution.py:77
  219.3 0.0 copy-done
  219.3 1.8 fusion.19
  221.1 0.0 all-gather.9.cloned.1.call-update
  221.2 0.0 all-gather.11.cloned.1.call-start
  221.9 0.0 copy-done.6
  221.9 0.6 fusion.28
  223.2 0.2 abs_reduce_fusion
  223.3 0.8 divide_convert_fusion
  224.1 0.0 all-gather.11.cloned.1.call-update
  224.1 0.0 reduce-scatter.5.cloned.1.call-start
  224.2 79.1 %all-gather.9.cloned.1.call-done = bf16[5120,512]{1,0:T(8,128)(2,1)} async-done(((bf16[320,512]{1,0:T(8,128)(2,1)}), bf16[5120,512]{1,0:T(8,128)(2,1)}) %all-gather.9.cloned.1.call-update) | async-done | bytes 5242896 | tf_op jit(solution)/shard_map/all_gather | solution.py:71
  303.3 12.4 %convolution_convert_fusion = bf16[5120,512]{1,0:T(8,128)(2,1)} fusion(f32[384]{0:T(512)S(1)} %add_rsqrt_fusion, bf16[1,2,384,5120]{3,2,1,0:T(8,128)(2,1)} %param.10, bf16[5120,512]{1,0:T(8,128)(2,1)} %all-gather.9.cloned.1.call-done, bf16[1,2,384,512]{3,2,1,0:T(8,128)(2,1)S(1)} %copy-done.5), kind=kOutput, calls=%fused_computation.8 | convolution fusion | flops 4043112448 | bytes 18747392 | tf_op jit(solution)/shard_map/dot_general | solution.py:78
  315.7 0.0 copy-start.7
  315.7 0.0 copy-start.2
  315.7 0.0 reduce-scatter.5.cloned.1.call-update
  315.8 35.2 %all-gather.2 = f32[16,20,128]{2,1,0:T(8,128)S(1)} all-gather(f32[1,20,128]{2,1,0:T(8,128)S(1)} %dynamic-slice_bitcast_fusion), channel_id=1, replica_groups=mesh['replica'=16,'fsdp'=16] {'replica'}, dimensions={0}, use_global_device_ids=true | all-gather | bytes 174080 | tf_op jit(solution)/shard_map/all_gather | solution.py:61
  351.0 0.0 copy-done.7
  351.0 0.6 dynamic-slice.1
  352.3 0.3 dynamic-update-slice
  352.5 74.1 %all-reduce = bf16[5120]{0:T(1024)(128)(2,1)S(1)} all-reduce(bf16[5120]{0:T(1024)(128)(2,1)S(1)} %dynamic-update-slice), channel_id=3, replica_groups=mesh['replica'=16,'fsdp'=16] {'replica'}, use_global_device_ids=true, to_apply=%add | all-reduce | flops 5120 | bytes 20480
  426.6 0.1 reshape.59
  426.8 0.0 all-gather.11.cloned.1.call-done
  426.8 1.9 fusion.4
  428.7 72.1 %reduce-scatter.5.cloned.1.call-done = bf16[320,512]{1,0:T(8,128)(2,1)} async-done(((bf16[5120,512]{1,0:T(8,128)(2,1)}), bf16[320,512]{1,0:T(8,128)(2,1)}) %reduce-scatter.5.cloned.1.call-update) | async-done | bytes 327696 | tf_op jit(solution)/shard_map/reduce_scatter | solution.py:77
  500.8 0.0 copy-done.2
  500.8 1.1 multiply_subtract_fusion
  502.0 0.1 bitcast_dynamic-update-slice_fusion
  502.1 0.0 copy-start.3
  502.1 0.1 multiply_add_fusion
  502.2 0.0 copy-start.1
  502.2 0.0 copy-start.4
  502.2 0.7 copy-done.3
  502.9 0.2 copy-done.1
  503.1 0.0 copy-done.4
  (9 shorter events, 0.1 us)
Async XLA Ops:
  7.2 91.8 %copy-start.5 = (bf16[1,2,384,512]{3,2,1,0:T(8,128)(2,1)S(1)}, bf16[1,2,384,512]{3,2,1,0:T(8,128)(2,1)}, u32[]{:S(2)}) copy-start(bf16[1,2,384,512]{3,2,1,0:T(8,128)(2,1)} %param.11) | copy-start | bytes 2359300
  7.2 91.8 %all-gather.7.cloned.1.call-start = ((), (), s32[]{:S(2)}) async-start(), calls=%async_computation.2 | async-start | bytes 5570560 | tf_op jit(solution)/shard_map/all_gather | solution.py:71
  11.0 208.3 %reduce-scatter.3.cloned.1.call-start = ((), (), s32[]{:S(2)}) async-start(), calls=%async_computation.3 | async-start | bytes 5570560 | tf_op jit(solution)/shard_map/reduce_scatter | solution.py:77
  111.4 108.0 %copy-start = (f32[1,320,512]{2,1,0:T(8,128)S(1)}, f32[1,320,512]{2,1,0:T(8,128)}, u32[]{:S(2)}) copy-start(f32[1,320,512]{2,1,0:T(8,128)} %param.7) | copy-start | bytes 1966084
  111.4 110.5 %copy-start.6 = (s32[8]{0:T(128)S(1)}, s32[8]{0:T(128)}, u32[]{:S(2)}) copy-start(s32[8]{0:T(128)} %param.13) | copy-start | bytes 100
  111.4 191.9 %all-gather.9.cloned.1.call-start = ((), (), s32[]{:S(2)}) async-start(), calls=%async_computation.4 | async-start | bytes 5570560 | tf_op jit(solution)/shard_map/all_gather | solution.py:71
  221.2 205.6 %all-gather.11.cloned.1.call-start = ((), (), s32[]{:S(2)}) async-start(), calls=%async_computation.6 | async-start | bytes 1392640 | tf_op jit(solution)/shard_map/all_gather | solution.py:54
  224.1 276.7 %reduce-scatter.5.cloned.1.call-start = ((), (), s32[]{:S(2)}) async-start(), calls=%async_computation.5 | async-start | bytes 5570560 | tf_op jit(solution)/shard_map/reduce_scatter | solution.py:77
  315.7 35.3 %copy-start.7 = (u32[256]{0:T(256)S(1)}, u32[256]{0:T(256)}, u32[]{:S(2)}) copy-start(u32[256]{0:T(256)} %constant.63) | copy-start | bytes 3076
  315.7 185.1 %copy-start.2 = (bf16[320,512]{1,0:T(8,128)(2,1)S(1)}, bf16[320,512]{1,0:T(8,128)(2,1)}, u32[]{:S(2)}) copy-start(bf16[320,512]{1,0:T(8,128)(2,1)} %reduce-scatter.3.cloned.1.call-done) | copy-start | bytes 983044
  502.1 0.8 copy-start.3
  502.2 1.0 copy-start.1
  502.2 0.9 copy-start.4
Sparse Core Ops, SparseCore 0:
  11.3 87.6 all-gather.6
  111.5 107.7 reduce-scatter.2
  222.6 80.6 all-gather.8
  305.5 73.0 all-gather.10
  382.9 117.8 reduce-scatter.4
where the time goes:
time: 510 us
  waiting for transfers between devices  343 us (67%)
  blocking collectives  109 us (21%)
  matrix products  24.8 us (5%)
  between operations  16 us (3%)
  other arithmetic  12.6 us (2%)
    reduce_scatter x2, waiting for transfers between devices, on_device(): lax.psum_scatter(jnp.dot(normed.T, slopes, preferred_element_type=jnp.flo...  180 us
    all_gather x2, waiting for transfers between devices, on_device(): lax.all_gather(weights.astype(jnp.bfloat16), 'fsdp', axis=0, tiled=True)  163 us
    unnamed x1, blocking collectives  74.1 us
    all_gather x1, blocking collectives, on_device(): moment_all = lax.all_gather(moment_cols, 'replica', axis=0, tiled=True)  35.2 us
    dot_general x2, matrix products, on_device(): jnp.dot(normed.T, slopes, preferred_element_type=jnp.float32)  24.8 us
  transfers between devices with their start and end apart: 5, of which 4 were waited for; matrix products, arithmetic and copies ran while one was open for 4% of the time, Pallas kernels for 0%

commit v1 on v0

--- a/solution.py
+++ b/solution.py
@@ -13,6 +13,13 @@
 outer_rate = 0.7
 outer_decay = 0.9
 mix_local = 0.5
+
+
+def exchange_gather(array, axis, dim):
+    size = lax.axis_size(axis)
+    tiles = jnp.stack([array for _ in range(size)])
+    tiles = lax.all_to_all(tiles, axis, split_axis=0, concat_axis=0)
+    return jnp.concatenate(tiles, axis=dim)
 
 
 def pick_fragment(step, plan):
@@ -68,7 +75,7 @@
         values = (
             jnp.dot(
                 normed,
-                lax.all_gather(weights.astype(jnp.bfloat16), "fsdp", axis=0, tiled=True),
+                exchange_gather(weights.astype(jnp.bfloat16), "fsdp", 0),
                 preferred_element_type=jnp.float32,
             )
             * inv_width

time: 510 us -> 575 us (1.13); the launches traced: 510 us -> 567 us
  waiting for transfers between devices: 343 us -> 374 us
  starting transfers between devices: 0.21 us -> 16.1 us
    all_to_all x0 -> x2, waiting for transfers between devices: none -> 261 us  [exchange_gather(): tiles = lax.all_to_all(tiles, axis, split_axis=0, concat_axis=0)]
    all_gather x2 -> x0, waiting for transfers between devices: 163 us -> none  [on_device(): lax.all_gather(weights.astype(jnp.bfloat16), 'fsdp', axis=0, tiled=True)]
    reduce_scatter x2, waiting for transfers between devices: 180 us -> 113 us  [on_device(): lax.psum_scatter(jnp.dot(normed.T, slopes, preferred_element_type=jnp.flo...]
    all_to_all x0 -> x2, starting transfers between devices: none -> 15.8 us  [exchange_gather(): tiles = lax.all_to_all(tiles, axis, split_axis=0, concat_axis=0)]
  transfers between devices with their start and end apart: 5 -> 5, of which waited for: 4 -> 3; matrix products, arithmetic and copies ran while one was open for 4% -> 4% of each run, Pallas kernels for 0% -> 0%
where the time goes in v1:
time: 575 us; the launch traced here: 567 us
  waiting for transfers between devices  374 us (65%)
  blocking collectives  113 us (20%)
  matrix products  24.9 us (4%)
  between operations  17.7 us (3%)
  starting transfers between devices  16.1 us (3%)
  other arithmetic  11.2 us (2%)
  local copies, waits for them, and re-layouts  9.57 us (2%)
    all_to_all x2, waiting for transfers between devices, exchange_gather(): tiles = lax.all_to_all(tiles, axis, split_axis=0, concat_axis=0)  261 us
    reduce_scatter x2, waiting for transfers between devices, on_device(): lax.psum_scatter(jnp.dot(normed.T, slopes, preferred_element_type=jnp.flo...  113 us
    unnamed x1, blocking collectives  78.4 us
    all_gather x1, blocking collectives, on_device(): moment_all = lax.all_gather(moment_cols, 'replica', axis=0, tiled=True)  34.9 us
    dot_general x2, matrix products, on_device(): jnp.dot(normed.T, slopes, preferred_element_type=jnp.float32)  24.9 us
    all_to_all x2, starting transfers between devices, exchange_gather(): tiles = lax.all_to_all(tiles, axis, split_axis=0, concat_axis=0)  15.8 us
  transfers between devices with their start and end apart: 5, of which 3 were waited for; matrix products, arithmetic and copies ran while one was open for 4% of the time, Pallas kernels for 0%

profile of v1, /device:TPU:8, one launch (start us, length us, event | category | flops | bytes accessed | tf_op | source)
XLA Modules:
  0.0 566.8 jit_solution(10662509239985618815)
XLA Ops:
  8.0 1.1 copy.17
  9.1 0.8 copy.18
  9.9 1.1 convert_bitcast_fusion.2
  11.0 2.9 stack.7
  13.9 11.1 %all-to-all-start = ((bf16[16,320,512]{2,1,0:T(8,128)(2,1)}), bf16[16,320,512]{2,1,0:T(8,128)(2,1)}, u32[]{:S(2)}, u32[]{:S(2)}) async-start(bf16[16,320,512]{2,1,0:T(8,128)(2,1)} %stack.7), calls=%async_computation | async-start | bytes 10485760 | tf_op jit(solution)/shard_map/all_to_all | solution.py:21
  24.9 0.0 copy-start.5
  25.0 0.0 reduce-scatter.3.cloned.1.call-start
  25.0 4.2 fusion.4
  29.2 117.1 %all-to-all-done = bf16[16,320,512]{2,1,0:T(8,128)(2,1)} async-done(((bf16[16,320,512]{2,1,0:T(8,128)(2,1)}), bf16[16,320,512]{2,1,0:T(8,128)(2,1)}, u32[]{:S(2)}, u32[]{:S(2)}) %all-to-all-start) | async-done | bytes 5242912 | tf_op jit(solution)/shard_map/all_to_all | solution.py:21
  146.3 0.0 copy-done.5
  146.3 12.5 %convolution_convert_fusion.1 = bf16[5120,512]{1,0:T(8,128)(2,1)} fusion(f32[384]{0:T(512)S(1)} %add_rsqrt_fusion.1, bf16[1,2,384,5120]{3,2,1,0:T(8,128)(2,1)} %param.10, bf16[5120,512]{1,0:T(8,128)(2,1)} %bitcast.5, bf16[1,2,384,512]{3,2,1,0:T(8,128)(2,1)S(1)} %copy-done.5), kind=kOutput, calls=%fused_computation.15 | convolution fusion | flops 4043112448 | bytes 18747392 | tf_op jit(solution)/shard_map/dot_general | solution.py:85
  158.8 0.0 copy-start
  158.8 0.0 reduce-scatter.3.cloned.1.call-update
  158.8 113.0 %reduce-scatter.3.cloned.1.call-done = bf16[320,512]{1,0:T(8,128)(2,1)} async-done(((bf16[5120,512]{1,0:T(8,128)(2,1)}), bf16[320,512]{1,0:T(8,128)(2,1)}) %reduce-scatter.3.cloned.1.call-update) | async-done | bytes 327696 | tf_op jit(solution)/shard_map/reduce_scatter | solution.py:84
  271.8 0.0 copy-done
  271.8 1.1 fusion.43
  272.9 2.9 stack.8
  275.8 0.0 copy-start.6
  275.8 4.7 all-to-all-start.1
  280.5 0.0 all-gather.5.cloned.1.call-start
  281.2 0.0 copy-done.6
  281.2 0.6 fusion.52
  282.5 0.2 abs_reduce_fusion
  282.6 0.8 divide_convert_fusion
  283.4 0.0 all-gather.5.cloned.1.call-update
  283.4 0.2 reduce-scatter.5.cloned.1.call-start
  283.7 143.9 %all-to-all-done.1 = bf16[16,320,512]{2,1,0:T(8,128)(2,1)} async-done(((bf16[16,320,512]{2,1,0:T(8,128)(2,1)}), bf16[16,320,512]{2,1,0:T(8,128)(2,1)}, u32[]{:S(2)}, u32[]{:S(2)}) %all-to-all-start.1) | async-done | bytes 5242912 | tf_op jit(solution)/shard_map/all_to_all | solution.py:21
  427.5 12.5 %convolution_convert_fusion = bf16[5120,512]{1,0:T(8,128)(2,1)} fusion(f32[384]{0:T(512)S(1)} %add_rsqrt_fusion, bf16[1,2,384,5120]{3,2,1,0:T(8,128)(2,1)} %param.10, bf16[5120,512]{1,0:T(8,128)(2,1)} %bitcast.9, bf16[1,2,384,512]{3,2,1,0:T(8,128)(2,1)S(1)} %copy-done.5), kind=kOutput, calls=%fused_computation.14 | convolution fusion | flops 4043112448 | bytes 18747392 | tf_op jit(solution)/shard_map/dot_general | solution.py:85
  440.0 0.0 copy-start.7
  440.0 0.0 copy-start.2
  440.0 0.0 reduce-scatter.5.cloned.1.call-update
  440.1 34.9 %all-gather.2 = f32[16,20,128]{2,1,0:T(8,128)S(1)} all-gather(f32[1,20,128]{2,1,0:T(8,128)S(1)} %dynamic-slice_bitcast_fusion), channel_id=1, replica_groups=mesh['replica'=16,'fsdp'=16] {'replica'}, dimensions={0}, use_global_device_ids=true | all-gather | bytes 174080 | tf_op jit(solution)/shard_map/all_gather | solution.py:68
  475.0 0.0 copy-done.7
  475.0 0.6 dynamic-slice.1
  476.2 0.3 dynamic-update-slice
  476.5 78.4 %all-reduce = bf16[5120]{0:T(1024)(128)(2,1)S(1)} all-reduce(bf16[5120]{0:T(1024)(128)(2,1)S(1)} %dynamic-update-slice), channel_id=3, replica_groups=mesh['replica'=16,'fsdp'=16] {'replica'}, use_global_device_ids=true, to_apply=%add | all-reduce | flops 5120 | bytes 20480
  554.9 0.1 reshape.86
  555.0 0.0 all-gather.5.cloned.1.call-done
  555.1 1.9 fusion.26
  557.0 0.0 reduce-scatter.5.cloned.1.call-done
  557.0 0.0 copy-done.2
  557.0 1.1 multiply_subtract_fusion
  558.2 0.1 bitcast_dynamic-update-slice_fusion
  558.3 0.0 copy-start.3
  558.3 0.1 multiply_add_fusion
  558.4 0.0 copy-start.1
  558.4 0.0 copy-start.4
  558.4 0.7 copy-done.3
  559.1 0.2 copy-done.1
  559.3 0.0 copy-done.4
  (9 shorter events, 0.1 us)
Async XLA Ops:
  13.9 132.4 %all-to-all-start = ((bf16[16,320,512]{2,1,0:T(8,128)(2,1)}), bf16[16,320,512]{2,1,0:T(8,128)(2,1)}, u32[]{:S(2)}, u32[]{:S(2)}) async-start(bf16[16,320,512]{2,1,0:T(8,128)(2,1)} %stack.7), calls=%async_computation | async-start | bytes 10485760 | tf_op jit(solution)/shard_map/all_to_all | solution.py:21
  24.9 121.4 %copy-start.5 = (bf16[1,2,384,512]{3,2,1,0:T(8,128)(2,1)S(1)}, bf16[1,2,384,512]{3,2,1,0:T(8,128)(2,1)}, u32[]{:S(2)}) copy-start(bf16[1,2,384,512]{3,2,1,0:T(8,128)(2,1)} %param.11) | copy-start | bytes 2359300
  25.0 246.9 %reduce-scatter.3.cloned.1.call-start = ((), (), s32[]{:S(2)}) async-start(), calls=%async_computation.4 | async-start | bytes 5570560 | tf_op jit(solution)/shard_map/reduce_scatter | solution.py:84
  158.8 113.1 %copy-start = (f32[1,320,512]{2,1,0:T(8,128)S(1)}, f32[1,320,512]{2,1,0:T(8,128)}, u32[]{:S(2)}) copy-start(f32[1,320,512]{2,1,0:T(8,128)} %param.7) | copy-start | bytes 1966084
  275.8 5.4 copy-start.6
  275.8 151.8 %all-to-all-start.1 = ((bf16[16,320,512]{2,1,0:T(8,128)(2,1)}), bf16[16,320,512]{2,1,0:T(8,128)(2,1)}, u32[]{:S(2)}, u32[]{:S(2)}) async-start(bf16[16,320,512]{2,1,0:T(8,128)(2,1)} %stack.8), calls=%async_computation.2 | async-start | bytes 10485760 | tf_op jit(solution)/shard_map/all_to_all | solution.py:21
  280.5 274.6 %all-gather.5.cloned.1.call-start = ((), (), s32[]{:S(2)}) async-start(), calls=%async_computation.6 | async-start | bytes 1392640 | tf_op jit(solution)/shard_map/all_gather | solution.py:61
  283.4 273.6 %reduce-scatter.5.cloned.1.call-start = ((), (), s32[]{:S(2)}) async-start(), calls=%async_computation.5 | async-start | bytes 5570560 | tf_op jit(solution)/shard_map/reduce_scatter | solution.py:84
  440.0 35.0 %copy-start.7 = (u32[256]{0:T(256)S(1)}, u32[256]{0:T(256)}, u32[]{:S(2)}) copy-start(u32[256]{0:T(256)} %constant.63) | copy-start | bytes 3076
  440.0 117.0 %copy-start.2 = (bf16[320,512]{1,0:T(8,128)(2,1)S(1)}, bf16[320,512]{1,0:T(8,128)(2,1)}, u32[]{:S(2)}) copy-start(bf16[320,512]{1,0:T(8,128)(2,1)} %reduce-scatter.3.cloned.1.call-done) | copy-start | bytes 983044
  558.3 0.8 copy-start.3
  558.4 1.0 copy-start.1
  558.4 0.9 copy-start.4
Sparse Core Ops, SparseCore 0:
  158.9 112.8 reduce-scatter.2
  440.2 109.0 reduce-scatter.4
Sparse Core Ops, SparseCore 1:
  283.5 92.4 all-gather.4
